TPU v7x, 128 devices: a whole 4x4x4 slice. The times are simulated.
128 devices in a mesh: row: 8 (over x_hi, y), col: 16 (over x_lo, z, core).
Axes of the slice: x: 4 (x_hi: 2, x_lo: 2; x = x_hi * 2 + x_lo), y: 4, z: 4, core: 2. Of those that a mesh axis runs over, the one named last changes fastest.
Arguments:
- vectors: float32 [100352, 2048], P(None, ('row', 'col')), may hold values from -6 to 6
- panels: float32 [2, 100352, 256], P(None, ('row', 'col')), may hold values from -0.078125 to 0.078125
- offsets: int32 [2], replicated, may hold values from 0 to 100096
- factor_upper: float32 [2, 256, 256], replicated, may hold values from -1 to 1
- scales: float32 [2, 256], replicated, may hold values from 1 to 2
Outputs:
- grid_vectors: float32 [100352, 2048], P('row', 'col')
All inputs are finite; a program needn't handle non-finite values.
Results may differ from a plain program's by a relative error of at most 0.00015.
Values sent between devices are 32-bit elements; how exact they have to be, the bound alone decides.
No kernel may reach another device: no remote copies, remote signals or barrier semaphores. Data moves between devices by JAX's collectives and lax.ppermute only.
A program may use at most 192 MiB of HBM per device.

v0:
```python
import jax
import jax.numpy as jnp
from jax import lax
from jax.sharding import PartitionSpec as P

NB = 64


def exact_dot(left, right):
    return jnp.dot(left, right, precision=lax.Precision.HIGHEST, preferred_element_type=jnp.float32)


def inner_dot(left, right):
    return lax.dot_general(
        left,
        right,
        (((0,), (0,)), ((), ())),
        precision=lax.Precision.HIGHEST,
        preferred_element_type=jnp.float32,
    )


def reflectors(panels, global_rows, offsets):
    width = panels.shape[2]
    begins = offsets[:, None, None] + jnp.arange(width, dtype=jnp.int32)[None, None, :]
    rows_at = global_rows[None, :, None]
    return jnp.where(
        rows_at < begins, jnp.float32(0.0), jnp.where(rows_at == begins, jnp.float32(1.0), panels)
    )


def build_factors(factor_upper, scales):
    width = factor_upper.shape[1]
    return jnp.triu(factor_upper, 1) + scales[:, :, None] * jnp.eye(width, dtype=jnp.float32)[None]


def matrix_rows(position, grid_rows, row_index):
    return (position // NB * grid_rows + row_index) * NB + position % NB


def shards(vectors, panels, offsets, factor_upper, scales):
    total_rows = vectors.shape[0]
    narrow = vectors.shape[1]
    grid_rows = lax.axis_size("row")
    local_rows = total_rows // grid_rows
    blocks = local_rows // NB
    factors = build_factors(factor_upper, scales)
    shaped = vectors.reshape(blocks, grid_rows, NB, narrow)
    moved = lax.all_to_all(shaped, "row", split_axis=1, concat_axis=1, tiled=True)
    current = moved.transpose(0, 2, 1, 3).reshape(local_rows, grid_rows * narrow)
    position = jnp.arange(local_rows, dtype=jnp.int32)
    whole = lax.all_gather(panels, "col", axis=1, tiled=True)
    reflect = reflectors(whole, matrix_rows(position, grid_rows, lax.axis_index("row")), offsets)
    for which in range(2):
        summed = lax.psum(inner_dot(reflect[which], current), "row")
        current = current - exact_dot(reflect[which], exact_dot(factors[which], summed))
    return current


def solution(mesh):
    return jax.shard_map(
        shards,
        mesh=mesh,
        in_specs=(P(None, ("row", "col")), P(None, ("row", "col"), None), P(), P(), P()),
        out_specs=P("row", "col"),
        check_vma=False,
    )
```

profile of v0, /device:TPU:0, one launch (start us, length us, event | category | flops | bytes accessed | tf_op | source)
XLA Modules:
  0.0 519.9 jit_solution(14125644273155514259)
XLA Ops:
  6.5 0.0 all-gather.2.cloned.1.call-start
  6.5 0.7 all-gather.2.cloned.1.call-update
  7.3 14.8 %reshape.60 = f32[196,8,64,16]{2,1,0,3:T(8,128)} reshape(f32[100352,16]{0,1:T(8,128)} %param.5) | data formatting | bytes 12845056 | tf_op jit(solution)/shard_map/reshape | solution.py:48
  22.0 10.9 %copy.9 = f32[196,8,64,16]{0,3,2,1:T(8,128)} copy(f32[196,8,64,16]{2,1,0,3:T(8,128)} %reshape.60) | data formatting | bytes 12845056 | tf_op jit(solution)/shard_map/reshape | solution.py:48
  33.0 0.0 copy-start.4
  33.0 7.1 %all-to-all-start = ((f32[196,8,64,16]{0,3,2,1:T(8,128)}), f32[196,8,64,16]{0,3,2,1:T(8,128)}, u32[]{:S(2)}, u32[]{:S(2)}) async-start(f32[196,8,64,16]{0,3,2,1:T(8,128)} %copy.9), calls=%async_computation | async-start | bytes 16777216 | tf_op jit(solution)/shard_map/all_to_all | solution.py:49
  40.0 0.4 all-reduce.3.cloned.1.call-start
  40.5 0.0 copy-done.4
  40.5 0.1 iota_add_fusion
  40.6 184.1 %all-to-all-done = f32[196,8,64,16]{0,3,2,1:T(8,128)} async-done(((f32[196,8,64,16]{0,3,2,1:T(8,128)}), f32[196,8,64,16]{0,3,2,1:T(8,128)}, u32[]{:S(2)}, u32[]{:S(2)}) %all-to-all-start) | async-done | bytes 6422560 | tf_op jit(solution)/shard_map/all_to_all | solution.py:49
  224.7 11.7 %copy.10 = f32[196,64,8,16]{1,0,3,2:T(8,128)} copy(f32[196,64,8,16]{0,3,1,2:T(8,128)} %bitcast) | data formatting | bytes 12845056 | tf_op jit(solution)/shard_map/transpose | solution.py:50
  236.4 10.5 %reshape.61 = f32[12544,128]{0,1:T(8,128)} reshape(f32[196,64,8,16]{1,0,3,2:T(8,128)} %copy.10) | data formatting | bytes 12845056 | tf_op jit(solution)/shard_map/reshape | solution.py:50
  246.9 9.6 %select_select_fusion = f32[2,12544,256]{2,1,0:T(8,128)S(1)} fusion(f32[2,12544,256]{2,1,0:T(8,128)} %all-gather.2.cloned.1.call-done, s32[2,256]{1,0:T(2,128)S(1)} %iota_add_fusion, s32[12544]{0:T(1024)S(1)} %fusion.14), kind=kLoop, calls=%fused_computation | loop fusion | flops 25690112 | bytes 51432448 | tf_op jit(solution)/shard_map/jit(_where)/select_n | solution.py:27
  256.5 0.0 copy-start
  256.5 8.5 %copy-done = f32[2,12544,256]{2,1,0:T(8,128)} copy-done((f32[2,12544,256]{2,1,0:T(8,128)}, f32[2,12544,256]{2,1,0:T(8,128)S(1)}, u32[]{:S(2)}) %copy-start) | copy-done | bytes 25690136
  265.0 22.9 %fusion = f32[256,128]{1,0:T(8,128)} fusion(f32[12544,128]{0,1:T(8,128)} %reshape.61, f32[2,12544,256]{2,1,0:T(8,128)S(1)} %select_select_fusion), kind=kOutput, calls=%fused_computation.5 | convolution fusion | flops 4932501504 | bytes 19398656 | tf_op jit(solution)/shard_map/dot_general | solution.py:14
  287.9 0.0 all-reduce.3.cloned.1.call-update
  287.9 12.1 %all-reduce.5.cloned.1.call-start = ((), (), s32[]{:S(2)}) async-start(), calls=%async_computation.3 | async-start | bytes 262144 | tf_op jit(solution)/shard_map/psum | solution.py:55
  300.0 0.0 copy-done.2
  300.1 0.0 copy-done.3
  300.1 0.1 multiply_add_fusion
  300.2 8.0 %copy.11 = f32[12544,128]{1,0:T(8,128)} copy(f32[12544,128]{0,1:T(8,128)} %reshape.61) | data formatting | bytes 12845056 | tf_op jit(solution)/shard_map/reshape | solution.py:50
  308.2 63.2 %all-reduce.3.cloned.1.call-done = f32[256,128]{1,0:T(8,128)} async-done(((f32[256,128]{1,0:T(8,128)}), f32[256,128]{1,0:T(8,128)}) %all-reduce.3.cloned.1.call-update) | async-done | bytes 131088 | tf_op jit(solution)/shard_map/psum | solution.py:55
  371.4 1.3 fusion.3
  372.6 14.4 %convolution_subtract_fusion.1 = f32[12544,128]{1,0:T(8,128)S(1)} fusion(f32[12544,128]{1,0:T(8,128)} %copy.11, f32[256,128]{1,0:T(8,128)S(1)} %fusion.3, f32[2,12544,256]{2,1,0:T(8,128)} %copy-done), kind=kOutput, calls=%fused_computation.2 | convolution fusion | flops 4934107136 | bytes 25821184 | tf_op jit(solution)/shard_map/dot_general | solution.py:10
  387.0 0.0 copy-start.1
  387.1 2.7 copy-done.1
  389.8 24.1 %fusion.1 = f32[256,128]{1,0:T(8,128)} fusion(f32[12544,128]{1,0:T(8,128)S(1)} %convolution_subtract_fusion.1, f32[2,12544,256]{2,1,0:T(8,128)} %copy-done), kind=kOutput, calls=%fused_computation.6 | convolution fusion | flops 4932501504 | bytes 19398656 | tf_op jit(solution)/shard_map/dot_general | solution.py:14
  413.9 0.0 all-reduce.5.cloned.1.call-update
  414.0 82.0 %all-reduce.5.cloned.1.call-done = f32[256,128]{1,0:T(8,128)} async-done(((f32[256,128]{1,0:T(8,128)}), f32[256,128]{1,0:T(8,128)}) %all-reduce.5.cloned.1.call-update) | async-done | bytes 131088 | tf_op jit(solution)/shard_map/psum | solution.py:55
  495.9 1.3 fusion.2
  497.2 16.0 %convolution_subtract_fusion = f32[12544,128]{1,0:T(8,128)} fusion(f32[12544,128]{1,0:T(8,128)} %copy-done.1, f32[256,128]{1,0:T(8,128)S(1)} %fusion.2, f32[2,12544,256]{2,1,0:T(8,128)} %copy-done), kind=kOutput, calls=%fused_computation.1 | convolution fusion | flops 4934107136 | bytes 25821184 | tf_op jit(solution)/shard_map/dot_general | solution.py:10
  (5 shorter events, 0.1 us)
Async XLA Ops:
  6.5 240.4 %all-gather.2.cloned.1.call-start = ((), (), s32[]{:S(2)}) async-start(), calls=%async_computation.1 | async-start | bytes 27295744 | tf_op jit(solution)/shard_map/all_gather | solution.py:52
  33.0 7.5 %copy-start.4 = (s32[2]{0:T(128)S(1)}, s32[2]{0:T(128)}, u32[]{:S(2)}) copy-start(s32[2]{0:T(128)} %param.7) | copy-start | bytes 28
  33.0 191.7 %all-to-all-start = ((f32[196,8,64,16]{0,3,2,1:T(8,128)}), f32[196,8,64,16]{0,3,2,1:T(8,128)}, u32[]{:S(2)}, u32[]{:S(2)}) async-start(f32[196,8,64,16]{0,3,2,1:T(8,128)} %copy.9), calls=%async_computation | async-start | bytes 16777216 | tf_op jit(solution)/shard_map/all_to_all | solution.py:49
  40.0 331.3 %all-reduce.3.cloned.1.call-start = ((), (), s32[]{:S(2)}) async-start(), calls=%async_computation.2 | async-start | bytes 262144 | tf_op jit(solution)/shard_map/psum | solution.py:55
  256.5 8.5 %copy-start = (f32[2,12544,256]{2,1,0:T(8,128)}, f32[2,12544,256]{2,1,0:T(8,128)S(1)}, u32[]{:S(2)}) copy-start(f32[2,12544,256]{2,1,0:T(8,128)S(1)} %select_select_fusion) | copy-start | bytes 77070336
  265.0 35.1 %copy-start.2 = (f32[2,256,256]{2,1,0:T(8,128)S(1)}, f32[2,256,256]{2,1,0:T(8,128)}, u32[]{:S(2)}) copy-start(f32[2,256,256]{2,1,0:T(8,128)} %param.8) | copy-start | bytes 1572868
  265.0 35.1 %copy-start.3 = (f32[2,256]{1,0:T(2,128)S(1)}, f32[2,256]{1,0:T(2,128)}, u32[]{:S(2)}) copy-start(f32[2,256]{1,0:T(2,128)} %param.9) | copy-start | bytes 6148
  287.9 208.0 %all-reduce.5.cloned.1.call-start = ((), (), s32[]{:S(2)}) async-start(), calls=%async_computation.3 | async-start | bytes 262144 | tf_op jit(solution)/shard_map/psum | solution.py:55
  387.0 2.7 copy-start.1
Sparse Core Ops, SparseCore 0:
  9.0 225.6 all-gather.1
  288.1 83.2 all-reduce.2
  414.1 81.7 all-reduce.4
where the time goes:
time: 524 us; the launch traced here: 520 us
  waiting for transfers between devices  330 us (63%)
  matrix products  80 us (15%)
  local copies, waits for them, and re-layouts  67.1 us (13%)
  starting transfers between devices  19.6 us (4%)
  between operations  13.4 us (3%)
  other arithmetic  9.84 us (2%)
    all_to_all x1, waiting for transfers between devices, shards(): lax.all_to_all(shaped, 'row', split_axis=1, concat_axis=1, tiled=True)  184 us
    psum x2, waiting for transfers between devices, shards(): summed = lax.psum(inner_dot(reflect[which], current), 'row')  145 us
    dot_general x2, matrix products, inner_dot(): lax.dot_general(left, right, (((0,), (0,)), ((), ())), precision=lax.Prec...  47.1 us
    dot_general x4, matrix products, exact_dot(): jnp.dot(left, right, precision=lax.Precision.HIGHEST, preferred_element_t...  32.9 us
    reshape x2, local copies, waits for them, and re-layouts, shards(): shaped = vectors.reshape(blocks, grid_rows, NB, narrow)  25.7 us
    reshape x2, local copies, waits for them, and re-layouts, shards(): moved.transpose(0, 2, 1, 3).reshape(local_rows, grid_rows * narrow)  18.5 us
    psum x2, starting transfers between devices, shards(): summed = lax.psum(inner_dot(reflect[which], current), 'row')  12.5 us
    transpose x1, local copies, waits for them, and re-layouts, shards(): moved.transpose(0, 2, 1, 3).reshape(local_rows, grid_rows * narrow)  11.7 us
  transfers between devices with their start and end apart: 4, of which 3 were waited for; matrix products, arithmetic and copies ran while one was open for 11% of the time, Pallas kernels for 0%

commit v1 on v0

v1 whole, which is shorter than its diff:
```python
import jax
import jax.numpy as jnp
from jax import lax
from jax.experimental import pallas as pl
from jax.experimental.pallas import tpu as pltpu
from jax.sharding import PartitionSpec as P

NB = 64
F32 = jnp.float32
BF16 = jnp.bfloat16


def exact_dot(left, right):
    return jnp.dot(left, right, precision=lax.Precision.HIGHEST, preferred_element_type=F32)


def build_factors(factor_upper, scales):
    width = factor_upper.shape[1]
    return jnp.triu(factor_upper, 1) + scales[:, :, None] * jnp.eye(width, dtype=F32)[None]


def split(value):
    high = value.astype(BF16)
    return high, (value - high.astype(F32)).astype(BF16)


def masked(block, offset, row_index, grid_rows, first):
    rows, width = block.shape
    position = first + lax.broadcasted_iota(jnp.int32, (rows, 1), 0)
    row = (position // NB * grid_rows + row_index) * NB + position % NB
    begin = offset + lax.broadcasted_iota(jnp.int32, (1, width), 1)
    return jnp.where(row < begin, 0.0, jnp.where(row == begin, 1.0, block))


def deal_kernel(in_ref, out_ref, *, pairs):
    lane = lax.broadcasted_iota(jnp.int32, (in_ref.shape[0], 128), 1)
    low = lane < NB
    for q in range(pairs):
        for t in range(4):
            a = in_ref[:, pl.ds(2 * q * 512 + t * 128, 128)]
            b = in_ref[:, pl.ds((2 * q + 1) * 512 + t * 128, 128)]
            out_ref[2 * t, :, pl.ds(q * 128, 128)] = jnp.where(low, a, pltpu.roll(b, NB, 1))
            out_ref[2 * t + 1, :, pl.ds(q * 128, 128)] = jnp.where(low, pltpu.roll(a, NB, 1), b)


def deal(vectors_t, grid_rows):
    narrow, total = vectors_t.shape
    local = total // grid_rows
    steps = 7
    return pl.pallas_call(
        lambda i, o: deal_kernel(i, o, pairs=local // 128 // steps),
        grid=(steps,),
        in_specs=[pl.BlockSpec((narrow, total // steps), lambda s: (0, s))],
        out_specs=pl.BlockSpec((grid_rows, narrow, local // steps), lambda s: (0, 0, s)),
        out_shape=jax.ShapeDtypeStruct((grid_rows, narrow, local), F32),
    )(vectors_t)


def inner_kernel(info, v_ref, r_ref, w_ref, o_ref, *, grid_rows):
    j = pl.program_id(0)
    rows = v_ref.shape[0]
    width = r_ref.shape[3]
    v_high, v_low = split(v_ref[...])
    both = jnp.concatenate([v_high, v_low], axis=1)
    narrow = v_ref.shape[1]

    @pl.when(j == 0)
    def _():
        o_ref[...] = w_ref[...]

    first = (info[3] * pl.num_programs(0) + j) * rows
    dims = (((0,), (0,)), ((), ()))
    for k in range(2):
        high, low = split(masked(r_ref[0, k], info[k], info[2], grid_rows, first))
        main = lax.dot_general(both, high, dims, preferred_element_type=F32)
        rest = lax.dot_general(v_high, low, dims, preferred_element_type=F32)
        o_ref[:, k * width : (k + 1) * width] += main[:narrow] + (main[narrow:] + rest)


def inner(info, v, gathered, start, grid_rows):
    count, panels, rows, width = gathered.shape
    narrow = v.shape[1]
    return pl.pallas_call(
        lambda *refs: inner_kernel(*refs, grid_rows=grid_rows),
        grid_spec=pltpu.PrefetchScalarGridSpec(
            num_scalar_prefetch=1,
            grid=(count,),
            in_specs=[
                pl.BlockSpec((rows, narrow), lambda j, s: (s[3] * count + j, 0)),
                pl.BlockSpec((1, panels, rows, width), lambda j, s: (j, 0, 0, 0)),
                pl.BlockSpec((narrow, panels * width), lambda j, s: (0, 0)),
            ],
            out_specs=pl.BlockSpec((narrow, panels * width), lambda j, s: (0, 0)),
        ),
        out_shape=jax.ShapeDtypeStruct((narrow, panels * width), F32),
        compiler_params=pltpu.CompilerParams(vmem_limit_bytes=48 * 1024 * 1024),
    )(info, v, gathered, start)


def solve_kernel(parts_ref, mix_ref, out_ref):
    total = parts_ref[0]
    for i in range(1, parts_ref.shape[0]):
        total += parts_ref[i]
    solved = jnp.dot(total, mix_ref[...], precision=lax.Precision.HIGHEST, preferred_element_type=F32)
    for i in range(parts_ref.shape[0]):
        out_ref[i] = solved


def solve(parts, mix):
    return pl.pallas_call(
        solve_kernel, out_shape=jax.ShapeDtypeStruct(parts.shape, F32)
    )(parts, mix)


def apply_kernel(info, v_ref, one_ref, two_ref, t_ref, o_ref, t_scr, *, grid_rows):
    h, j = pl.program_id(0), pl.program_id(1)
    rows, narrow = v_ref.shape
    width = one_ref.shape[3]

    @pl.when((h == 0) & (j == 0))
    def _():
        for k in range(2):
            high, low = split(t_ref[:, k * width : (k + 1) * width].T)
            t_scr[k, :, :narrow] = high
            t_scr[k, :, narrow:] = low

    half = jnp.where(h == 0, info[3], 1 - info[3])
    first = (half * pl.num_programs(1) + j) * rows

    def run(r_ref):
        total = v_ref[...]
        for k in range(2):
            high, low = split(masked(r_ref[0, k], info[k], info[2], grid_rows, first))
            main = jnp.dot(high, t_scr[k], preferred_element_type=F32)
            rest = jnp.dot(low, t_scr[k, :, :narrow], preferred_element_type=F32)
            total -= main[:, :narrow] + (main[:, narrow:] + rest)
        o_ref[...] = total

    @pl.when(h == 0)
    def _():
        run(one_ref)

    @pl.when(h == 1)
    def _():
        run(two_ref)


def apply(info, v, one, two, t, grid_rows):
    count, panels, rows, width = one.shape
    narrow = v.shape[1]

    def place(h, j, s):
        return (jnp.where(h == 0, s[3], 1 - s[3]) * count + j, 0)

    return pl.pallas_call(
        lambda *refs: apply_kernel(*refs, grid_rows=grid_rows),
        grid_spec=pltpu.PrefetchScalarGridSpec(
            num_scalar_prefetch=1,
            grid=(2, count),
            in_specs=[
                pl.BlockSpec((rows, narrow), place),
                pl.BlockSpec((1, panels, rows, width), lambda h, j, s: (jnp.where(h == 0, j, count - 1), 0, 0, 0)),
                pl.BlockSpec((1, panels, rows, width), lambda h, j, s: (jnp.where(h == 0, 0, j), 0, 0, 0)),
                pl.BlockSpec((narrow, panels * width), lambda h, j, s: (0, 0)),
            ],
            out_specs=pl.BlockSpec((rows, narrow), place),
            scratch_shapes=[pltpu.VMEM((panels, width, 2 * narrow), BF16)],
        ),
        out_shape=jax.ShapeDtypeStruct(v.shape, F32),
        compiler_params=pltpu.CompilerParams(vmem_limit_bytes=48 * 1024 * 1024),
    )(info, v, one, two, t)


def shards(vectors, panels, offsets, factor_upper, scales):
    grid_rows, grid_cols = lax.axis_size("row"), lax.axis_size("col")
    row_index, col_index = lax.axis_index("row"), lax.axis_index("col")
    everyone = grid_rows * grid_cols
    half = grid_cols // 2
    rows, width = panels.shape[1:]
    narrow = vectors.shape[1]
    groups = [list(range(half)), list(range(half, grid_cols))]
    side = col_index // half

    other = lax.ppermute(panels, "col", [(c, c ^ half) for c in range(grid_cols)])
    one = lax.all_gather(panels, "col", axis=0, axis_index_groups=groups)
    two = lax.all_gather(other, "col", axis=0, axis_index_groups=groups)

    reflect = [masked(panels[k], offsets[k], row_index, grid_rows, col_index * rows) for k in range(2)]
    gram = exact_dot(reflect[1].T, reflect[0])
    gram = lax.all_to_all(gram.reshape(everyone, width // everyone, width), ("row", "col"), 0, 0, tiled=True).sum(0)
    gram = lax.all_to_all(jnp.broadcast_to(gram[None], (everyone,) + gram.shape), ("row", "col"), 0, 0, tiled=True)
    gram = gram.reshape(width, width)
    factors = build_factors(factor_upper, scales)
    corner = exact_dot(factors[1], exact_dot(gram, factors[0]))
    mix = jnp.concatenate(
        [
            jnp.concatenate([factors[0].T, -corner.T], axis=1),
            jnp.concatenate([jnp.zeros((width, width), F32), factors[1].T], axis=1),
        ],
        axis=0,
    )

    dealt = deal(vectors.T, grid_rows)
    dealt, other = lax.optimization_barrier((dealt, other))
    moved = lax.all_to_all(dealt, "row", 0, 0, tiled=True)
    current = moved.reshape(grid_rows * narrow, -1).T

    def info(which):
        return jnp.stack([offsets[0], offsets[1], row_index.astype(jnp.int32), which.astype(jnp.int32)])

    start = jnp.zeros((grid_rows * narrow, 2 * width), F32)
    sums = inner(info(side), current, one, start, grid_rows)
    sums = inner(info(1 - side), current, two, sums, grid_rows)
    parts = lax.all_to_all(sums.reshape(grid_rows, narrow, 2 * width), "row", 0, 0, tiled=True)
    solved = solve(parts, mix)
    solved = lax.all_to_all(solved, "row", 0, 0, tiled=True).reshape(grid_rows * narrow, 2 * width)
    return apply(info(side), current, one, two, solved, grid_rows)


def solution(mesh):
    return jax.shard_map(
        shards,
        mesh=mesh,
        in_specs=(P(None, ("row", "col")), P(None, ("row", "col"), None), P(), P(), P()),
        out_specs=P("row", "col"),
        check_vma=False,
    )
```

time: 524 us -> 265 us (0.51)
  waiting for transfers between devices: 330 us -> 117 us
  matrix products: 80 us -> 2.17 us
  Pallas kernels: 0 us -> 63.4 us
  local copies, waits for them, and re-layouts: 67.1 us -> 13.4 us
  blocking collectives: 0 us -> 34 us
  other arithmetic: 9.84 us -> 3.99 us
    psum x2 -> x0, waiting for transfers between devices: 145 us -> none  [shards(): summed = lax.psum(inner_dot(reflect[which], current), 'row')]
    all_to_all x1 -> x3, waiting for transfers between devices: 184 us -> 81.3 us  [the longest x1 72.2 us: shards(): moved = lax.all_to_all(dealt, 'row', 0, 0, tiled=True)]
    pallas_call x0 -> x5, Pallas kernels: none -> 63.4 us  [the longest x2 27.2 us: inner(): pl.pallas_call(lambda *refs: inner_kernel(*refs, grid_rows=grid_rows), gr...]
    dot_general x2 -> x0, matrix products: 47.1 us -> none  [inner_dot(): lax.dot_general(left, right, (((0,), (0,)), ((), ())), precision=lax.Prec...]
    reshape x4 -> x2, local copies, waits for them, and re-layouts: 44.2 us -> 8.11 us  [the longest x1 7.93 us: shards(): current = moved.reshape(grid_rows * narrow, -1).T]
    ppermute x0 -> x1, waiting for transfers between devices: none -> 35.3 us  [shards(): lax.ppermute(panels, 'col', [(c, c ^ half) for c in range(grid_cols)])]
    all_to_all x0 -> x2, blocking collectives: none -> 34 us  [the longest x1 21.9 us: shards(): lax.all_to_all(gram.reshape(everyone, width // everyone, width), ('row',...]
    dot_general x4 -> x3, matrix products: 32.9 us -> 2.17 us  [exact_dot(): jnp.dot(left, right, precision=lax.Precision.HIGHEST, preferred_element_t...]
  transfers between devices with their start and end apart: 4 -> 6, of which waited for: 3 -> 4; matrix products, arithmetic and copies ran while one was open for 11% -> 7% of each run, Pallas kernels for 0% -> 8%
where the time goes in v1:
time: 265 us; the launch traced here: 264 us
  waiting for transfers between devices  117 us (44%)
  Pallas kernels  63.4 us (24%)
  blocking collectives  34 us (13%)
  starting transfers between devices  15.8 us (6%)
  between operations  13.6 us (5%)
  local copies, waits for them, and re-layouts  13.4 us (5%)
  other arithmetic  3.99 us (2%)
    all_to_all x1, waiting for transfers between devices, shards(): moved = lax.all_to_all(dealt, 'row', 0, 0, tiled=True)  72.2 us
    ppermute x1, waiting for transfers between devices, shards(): lax.ppermute(panels, 'col', [(c, c ^ half) for c in range(grid_cols)])  35.3 us
    pallas_call x2, Pallas kernels, inner(): pl.pallas_call(lambda *refs: inner_kernel(*refs, grid_rows=grid_rows), gr...  27.2 us
    pallas_call x1, Pallas kernels, apply(): pl.pallas_call(lambda *refs: apply_kernel(*refs, grid_rows=grid_rows), gr...  24.7 us
    all_to_all x1, blocking collectives, shards(): lax.all_to_all(gram.reshape(everyone, width // everyone, width), ('row',...  21.9 us
    all_to_all x1, blocking collectives, shards(): lax.all_to_all(solved, 'row', 0, 0, tiled=True)  12 us
    pallas_call x1, Pallas kernels, deal(): pl.pallas_call(lambda i, o: deal_kernel(i, o, pairs=local // 128 // steps...  8.92 us
    reshape x1, local copies, waits for them, and re-layouts, shards(): current = moved.reshape(grid_rows * narrow, -1).T  7.93 us
  transfers between devices with their start and end apart: 6, of which 4 were waited for; matrix products, arithmetic and copies ran while one was open for 7% of the time, Pallas kernels for 8%

profile of v1, /device:TPU:0, one launch (start us, length us, event | category | flops | bytes accessed | tf_op | source)
XLA Modules:
  0.0 263.6 jit_solution(13060130906741039965)
XLA Ops:
  6.5 0.7 all-gather.5.cloned.1.call-update
  7.3 1.7 collective-permute-start
  9.0 35.3 %collective-permute-done = f32[2,784,256]{2,1,0:T(8,128)S(1)} collective-permute-done((f32[2,784,256]{2,1,0:T(8,128)}, f32[2,784,256]{2,1,0:T(8,128)S(1)}, u32[]{:S(2)}, u32[]{:S(2)}) %collective-permute-start) | collective-permute-done | bytes 1605664 | tf_op jit(solution)/shard_map/ppermute | solution.py:184
  44.3 1.1 copy-done.1
  45.4 1.3 fusion.31
  46.8 0.6 iota_add_fusion.2
  47.3 1.3 fusion.4
  48.7 0.3 copy.17
  49.0 0.5 dot_general.14
  49.5 0.7 iota_add_fusion.1
  50.2 1.2 fusion
  51.4 0.2 copy.19
  51.6 21.9 %all_to_all.25 = f32[128,2,256]{2,1,0:T(2,128)S(1)} all-to-all(f32[128,2,256]{2,1,0:T(2,128)S(1)} %copy.19), channel_id=1, replica_groups=mesh['row'=8,'col'=16] {'row','col'}, dimensions={0} | all-to-all | bytes 524288 | tf_op jit(solution)/shard_map/all_to_all | solution.py:190
  73.6 0.8 broadcast_in_dim.40
  74.4 4.5 %all-to-all-start.3 = ((f32[128,2,256]{2,1,0:T(2,128)}), f32[128,2,256]{2,1,0:T(2,128)S(1)}, u32[]{:S(2)}, u32[]{:S(2)}) async-start(f32[128,2,256]{2,1,0:T(2,128)} %broadcast_in_dim.40), calls=%async_computation.3 | async-start | bytes 524288 | tf_op jit(solution)/shard_map/all_to_all | solution.py:191
  79.0 8.9 %shard_map.55 = f32[8,16,12544]{2,1,0:T(8,128)} custom-call(f32[16,100352]{1,0:T(8,128)} %bitcast.46), custom_call_target="tpu_custom_call" | custom-call | tf_op jit(solution)/shard_map/pallas_call | solution.py:50
  87.9 1.9 all-to-all-done.3
  89.8 4.8 %all-to-all-start = ((f32[8,16,12544]{2,1,0:T(8,128)}), f32[8,16,12544]{2,1,0:T(8,128)}, u32[]{:S(2)}, u32[]{:S(2)}) async-start(f32[8,16,12544]{2,1,0:T(8,128)} %shard_map.55), calls=%async_computation | async-start | bytes 12845056 | tf_op jit(solution)/shard_map/all_to_all | solution.py:205
  94.6 0.2 copy.16
  95.3 0.4 fusion.15
  95.7 72.2 %all-to-all-done = f32[8,16,12544]{2,1,0:T(8,128)} async-done(((f32[8,16,12544]{2,1,0:T(8,128)}), f32[8,16,12544]{2,1,0:T(8,128)}, u32[]{:S(2)}, u32[]{:S(2)}) %all-to-all-start) | async-done | bytes 6422560 | tf_op jit(solution)/shard_map/all_to_all | solution.py:205
  167.9 7.9 %copy.15 = f32[128,12544]{0,1:T(8,128)} copy(f32[128,12544]{1,0:T(8,128)} %bitcast.3) | data formatting | bytes 12845056 | tf_op jit(solution)/shard_map/reshape | solution.py:206
  175.8 13.2 %shard_map.56.refs_3_ = f32[128,512]{1,0:T(8,128)S(1)} custom-call(s32[4]{0:T(128)S(1)} %get-tuple-element.12.refs_0_, f32[12544,128]{1,0:T(8,128)} %bitcast.39, f32[8,2,784,256]{3,2,1,0:T(8,128)} %bitcast.42, f32[128,512]{1,0:T(8,128)S(1)} %broadcast_in_dim.33.refs_3_), custom_call_target="tpu_custom_call" | custom-call | tf_op jit(solution)/shard_map/pallas_call | solution.py:83
  189.1 13.9 %shard_map.57 = f32[128,512]{1,0:T(8,128)} custom-call(s32[4]{0:T(128)S(1)} %get-tuple-element.11.refs_0_, f32[12544,128]{1,0:T(8,128)} %bitcast.40, f32[8,2,784,256]{3,2,1,0:T(8,128)} %bitcast.44, f32[128,512]{1,0:T(8,128)S(1)} %shard_map.56.refs_3_), custom_call_target="tpu_custom_call" | custom-call | tf_op jit(solution)/shard_map/pallas_call | solution.py:83
  203.0 4.7 %all-to-all-start.1 = ((f32[8,16,512]{2,1,0:T(8,128)}), f32[8,16,512]{2,1,0:T(8,128)S(1)}, u32[]{:S(2)}, u32[]{:S(2)}) async-start(f32[8,16,512]{2,1,0:T(8,128)} %bitcast.8), calls=%async_computation.1 | async-start | bytes 524288 | tf_op jit(solution)/shard_map/all_to_all | solution.py:214
  207.8 0.6 convolution_negate_fusion
  208.4 1.1 select_maximum_fusion.mix_ref
  209.5 7.2 %all-to-all-done.1.parts_ref = f32[8,16,512]{2,1,0:T(8,128)S(1)} async-done(((f32[8,16,512]{2,1,0:T(8,128)}), f32[8,16,512]{2,1,0:T(8,128)S(1)}, u32[]{:S(2)}, u32[]{:S(2)}) %all-to-all-start.1) | async-done | bytes 262176 | tf_op jit(solution)/shard_map/all_to_all | solution.py:214
  216.7 0.7 copy-done.2
  217.4 2.6 shard_map.58
  220.0 12.0 %all_to_all.26 = f32[8,16,512]{2,1,0:T(8,128)S(1)} all-to-all(f32[8,16,512]{2,1,0:T(8,128)} %shard_map.58), channel_id=1, replica_groups=mesh['row'=8,'col'=16] {'row'}, dimensions={0} | all-to-all | bytes 524288 | tf_op jit(solution)/shard_map/all_to_all | solution.py:216
  232.1 24.7 %shard_map.59 = f32[12544,128]{1,0:T(8,128)} custom-call(s32[4]{0:T(128)S(1)} %get-tuple-element.12.refs_0_, f32[12544,128]{1,0:T(8,128)} %bitcast.41, f32[8,2,784,256]{3,2,1,0:T(8,128)} %bitcast.43, f32[8,2,784,256]{3,2,1,0:T(8,128)} %bitcast.45, f32[128,512]{1,0:T(8,128)S(1)} %bitcast.38), custom_call_target="tpu_custom_call" | custom-call | tf_op jit(solution)/shard_map/pallas_call | solution.py:155
  (23 shorter events, 0.7 us)
Async XLA Ops:
  6.5 43.6 %copy-start = (f32[2,784,256]{2,1,0:T(8,128)S(1)}, f32[2,784,256]{2,1,0:T(8,128)}, u32[]{:S(2)}) copy-start(f32[2,784,256]{2,1,0:T(8,128)} %param.6) | copy-start | bytes 4816900
  6.5 169.3 %all-gather.5.cloned.1.call-start = ((), (), s32[]{:S(2)}) async-start(), calls=%async_computation.5 | async-start | bytes 14450688 | tf_op jit(solution)/shard_map/all_gather | solution.py:185
  7.3 181.8 %all-gather.7.cloned.1.call-start = ((), (), s32[]{:S(2)}) async-start(), calls=%async_computation.6 | async-start | bytes 14450688 | tf_op jit(solution)/shard_map/all_gather | solution.py:186
  7.3 37.0 %collective-permute-start = (f32[2,784,256]{2,1,0:T(8,128)}, f32[2,784,256]{2,1,0:T(8,128)S(1)}, u32[]{:S(2)}, u32[]{:S(2)}) collective-permute-start(f32[2,784,256]{2,1,0:T(8,128)} %param.6), channel_id=1, source_target_pairs={{0,8},{1,9},{2,10},{3,11},{4,12},{5,13},{6,14},{7,15},{8,0},{9,1},... | collective-permute-start | bytes 4816904 | tf_op jit(solution)/shard_map/ppermute | solution.py:184
  44.3 1.1 copy-start.1
  74.4 15.3 %all-to-all-start.3 = ((f32[128,2,256]{2,1,0:T(2,128)}), f32[128,2,256]{2,1,0:T(2,128)S(1)}, u32[]{:S(2)}, u32[]{:S(2)}) async-start(f32[128,2,256]{2,1,0:T(2,128)} %broadcast_in_dim.40), calls=%async_computation.3 | async-start | bytes 524288 | tf_op jit(solution)/shard_map/all_to_all | solution.py:191
  87.9 6.7 %copy-start.3 = (f32[2,256,256]{2,1,0:T(8,128)S(1)}, f32[2,256,256]{2,1,0:T(8,128)}, u32[]{:S(2)}) copy-start(f32[2,256,256]{2,1,0:T(8,128)} %param.8) | copy-start | bytes 1572868
  87.9 6.9 %copy-start.4 = (s32[2]{0:T(128)S(1)}, s32[2]{0:T(128)}, u32[]{:S(2)}) copy-start(s32[2]{0:T(128)} %param.7) | copy-start | bytes 28
  87.9 7.0 %copy-start.5 = (f32[2,256]{1,0:T(2,128)S(1)}, f32[2,256]{1,0:T(2,128)}, u32[]{:S(2)}) copy-start(f32[2,256]{1,0:T(2,128)} %param.9) | copy-start | bytes 6148
  89.8 78.1 %all-to-all-start = ((f32[8,16,12544]{2,1,0:T(8,128)}), f32[8,16,12544]{2,1,0:T(8,128)}, u32[]{:S(2)}, u32[]{:S(2)}) async-start(f32[8,16,12544]{2,1,0:T(8,128)} %shard_map.55), calls=%async_computation | async-start | bytes 12845056 | tf_op jit(solution)/shard_map/all_to_all | solution.py:205
  203.0 13.7 %all-to-all-start.1 = ((f32[8,16,512]{2,1,0:T(8,128)}), f32[8,16,512]{2,1,0:T(8,128)S(1)}, u32[]{:S(2)}, u32[]{:S(2)}) async-start(f32[8,16,512]{2,1,0:T(8,128)} %bitcast.8), calls=%async_computation.1 | async-start | bytes 524288 | tf_op jit(solution)/shard_map/all_to_all | solution.py:214
  216.7 0.7 copy-start.2
Sparse Core Ops, SparseCore 0:
  9.0 73.9 all-gather.4
  84.7 68.8 all-gather.6
